TPU v7x, 128 devices: a whole 4x4x4 slice. The times are simulated.
128 devices in a mesh: outer: 8 (over z, core), inner: 16 (over x, y).
Axes of the slice: x: 4, y: 4, z: 4, core: 2. Of those that a mesh axis runs over, the one named last changes fastest.
Arguments:
- signal: float32 [65536, 512], P(('outer', 'inner')), may hold values from -6 to 6
- spectrum: float32 [128, 2, 512, 256], P(('outer', 'inner')), may hold values from -6 to 6
- skip_gain: float32 [512], replicated, may hold values from 0.5 to 1.5
Outputs:
- output: float32 [65536, 512], P(('outer', 'inner'))
All inputs are finite; a program needn't handle non-finite values.
Results may differ from a plain program's by a relative error of at most 0.000059.
Values sent between devices are 32-bit elements; how exact they have to be, the bound alone decides.
A program may use at most 64 MiB of HBM per device.

v0:
```python
import functools
import math

import jax
import jax.numpy as jnp
import ml_dtypes
import numpy as np
from jax import lax
from jax.experimental import pallas as pl
from jax.experimental.pallas import tpu as pltpu
from jax.sharding import PartitionSpec as P

F32 = jnp.float32
BF16 = jnp.bfloat16
LANES = 128
STEP = 21


def halves(table):
    high = table.astype(ml_dtypes.bfloat16)
    low = (table - high.astype(np.float64)).astype(ml_dtypes.bfloat16)
    return high, low


def tables(blocks, seq_len):
    slots = blocks // 2
    total = blocks * seq_len
    d = np.arange(blocks)
    s = np.arange(slots)
    m = np.arange(seq_len)
    angle = 2.0 * math.pi / blocks * (s[:, None] * d[None, :] % blocks)
    cos_rows = np.cos(angle)
    sin_rows = np.sin(angle)
    sin_rows[0] = np.where(d % 2 == 0, -1.0, 1.0)
    fwd = np.concatenate([cos_rows, -sin_rows], 0)
    scale = np.where(s == 0, 1.0, 2.0)[:, None] / total
    minus = sin_rows * scale
    minus[0] = np.where(d % 2 == 0, 1.0, -1.0) * scale[0]
    inv = np.concatenate([cos_rows * scale, minus], 0).T
    turn = 2.0 * math.pi / total * (np.arange(slots + 1)[:, None] * m[None, :] % total)
    twiddle = np.stack([np.cos(turn[:slots]), np.sin(turn[:slots])]).astype(np.float32)
    middle = np.stack([np.cos(turn[slots]), np.sin(turn[slots])]).astype(np.float32)
    middle = np.concatenate([middle, np.zeros((6, seq_len), np.float32)], 0)
    theta = 2.0 * math.pi / seq_len * (m[:, None] * m[None, :] % seq_len)
    cos_t = np.cos(theta)
    sin_t = np.sin(theta)
    dft = np.concatenate(
        [np.concatenate([cos_t, -sin_t], 1), np.concatenate([sin_t, cos_t], 1)], 0
    )
    fwd_hl = np.stack(halves(fwd))
    inv_hl = np.stack(halves(inv))
    dft_hl = np.stack(halves(dft))
    return fwd_hl, inv_hl, dft_hl, twiddle, middle


def split(value):
    high = value.astype(BF16)
    return high, (value - high.astype(F32)).astype(BF16)


def mm(left, right):
    return jnp.dot(left, right, preferred_element_type=F32)


def table_dot(table_ref, value):
    high, low = split(value)
    return mm(table_ref[0], high) + mm(table_ref[0], low) + mm(table_ref[1], high)


def dft_dot(rows, dft_ref):
    high, low = split(rows)
    return mm(high, dft_ref[0]) + mm(low, dft_ref[0]) + mm(high, dft_ref[1])


def kernel(
    blocks,
    inner,
    signal_hbm,
    spectrum_hbm,
    dft_hbm,
    fwd_hbm,
    inv_hbm,
    twiddle_hbm,
    middle_hbm,
    out_ref,
    signal,
    spectrum,
    dft,
    fwd,
    inv,
    twiddle,
    middle,
    send_x,
    recv_x,
    send_f,
    recv_f,
    send_y,
    recv_y,
    stack,
    bins,
    load_sem,
    x_sem,
    f_sem,
    y_sem,
):
    me = lax.axis_index("outer") * inner + lax.axis_index("inner")
    slots = blocks // 2
    seq_len = signal.shape[0]
    m_tiles = seq_len // LANES
    half_rows = stack.shape[0] // 2

    loads = []
    for i, (src, dst) in enumerate(
        (
            (signal_hbm, signal),
            (spectrum_hbm, spectrum),
            (fwd_hbm, fwd),
            (twiddle_hbm, twiddle),
            (middle_hbm, middle),
            (dft_hbm, dft),
            (inv_hbm, inv),
        )
    ):
        copy = pltpu.make_async_copy(src, dst, load_sem.at[i])
        copy.start()
        loads.append(copy)

    def partner(k):
        p = lax.rem(me + lax.rem(k * STEP, blocks), blocks)
        return p, (p // inner, lax.rem(p, inner))

    barrier = pltpu.get_barrier_semaphore()

    @pl.loop(1, blocks)
    def _(k):
        _, device = partner(k)
        pl.semaphore_signal(
            barrier, inc=1, device_id=device, device_id_type=pl.DeviceIdType.MESH
        )

    def exchange(src, dst, rows, sems):
        @pl.loop(1, blocks)
        def _(k):
            p, device = partner(k)
            pltpu.make_async_remote_copy(
                src_ref=src.at[pl.ds(pl.multiple_of(p * rows, rows), rows)],
                dst_ref=dst.at[pl.ds(pl.multiple_of(me * rows, rows), rows)],
                send_sem=sems.at[0],
                recv_sem=sems.at[1],
                device_id=device,
                device_id_type=pl.DeviceIdType.MESH,
            ).start()

        own = pl.ds(pl.multiple_of(me * rows, rows), rows)
        dst[own, :] = src[own, :]

    def wait_all(ref, rows, sem):
        part = ref.at[pl.ds(0, (blocks - 1) * rows)]
        pltpu.make_async_copy(part, part, sem).wait()

    loads[0].wait()
    chan_tiles = signal.shape[1] // LANES
    x_rows = chan_tiles * m_tiles
    for ct in range(chan_tiles):
        for mt in range(m_tiles):
            tile = signal[mt * LANES : (mt + 1) * LANES, ct * LANES : (ct + 1) * LANES]
            send_x[pl.ds(ct * m_tiles + mt, LANES, stride=x_rows), :] = tile.T
    pl.semaphore_wait(barrier, blocks - 1)
    exchange(send_x, recv_x, x_rows, x_sem)

    loads[1].wait()
    f_rows = 2 * m_tiles
    for g in range(2):
        for r in range(2):
            for bt in range(m_tiles):
                tile = spectrum[
                    r, bt * LANES : (bt + 1) * LANES, g * LANES : (g + 1) * LANES
                ]
                send_f[g, pl.ds(r * m_tiles + bt, LANES, stride=f_rows), :] = tile.T
        exchange(send_f.at[g], recv_f.at[g], f_rows, f_sem.at[g])

    for copy in loads[2:]:
        copy.wait()
    first = lax.broadcasted_iota(jnp.int32, (slots, seq_len), 0) == 0

    wait_all(recv_x, x_rows, x_sem.at[1])
    for g in range(2):
        base = g * half_rows
        extra = []
        for h in range(2):
            ct = 2 * h + g
            data = jnp.concatenate(
                [
                    recv_x[pl.ds(ct * m_tiles + mt, blocks, stride=x_rows), :]
                    for mt in range(m_tiles)
                ],
                1,
            )
            packed = table_dot(fwd, data)
            re = packed[:slots]
            im = packed[slots:]
            cos_t = twiddle[0]
            sin_t = twiddle[1]
            rows = pl.ds(base + h * slots, slots)
            stack[rows, :seq_len] = re * cos_t + im * sin_t
            stack[rows, seq_len:] = jnp.where(first, 0.0, im * cos_t - re * sin_t)
            extra.append(im[0:1])
        pad = jnp.zeros((half_rows - 2 * slots - 2, seq_len), F32)
        middle_in = jnp.concatenate([*extra, pad], 0)
        rows = pl.ds(base + 2 * slots, half_rows - 2 * slots)
        stack[rows, :seq_len] = middle_in * middle[0:1]
        stack[rows, seq_len:] = -middle_in * middle[1:2]
    bins[...] = dft_dot(stack[...], dft)

    lane = lax.broadcasted_iota(jnp.int32, (1, LANES), 1)
    for g in range(2):
        base = g * half_rows
        wait_all(recv_f.at[g], f_rows, f_sem.at[g, 1])
        mid_re = []
        mid_im = []
        for h in range(2):
            rows = pl.ds(base + h * slots, slots)
            f_re = [
                recv_f[g, pl.ds(h * f_rows + bt, slots, stride=2 * f_rows), :]
                for bt in range(m_tiles)
            ]
            f_im = [
                recv_f[g, pl.ds(h * f_rows + m_tiles + bt, slots, stride=2 * f_rows), :]
                for bt in range(m_tiles)
            ]
            top_re = [t[0:1] for t in f_re]
            top_im = [t[0:1] for t in f_im]
            half = m_tiles // 2
            zero = jnp.zeros((1, LANES), F32)
            base_re = [2.0 * t for t in top_re[:half]] + [zero] * half
            base_im = [2.0 * t for t in top_im[:half]] + [zero] * half
            base_re[0] = jnp.where(lane == 0, top_re[0], base_re[0])
            base_im[0] = jnp.where(lane == 0, 0.0, base_im[0])
            base_re[half] = jnp.where(lane == 0, top_im[0], 0.0)
            mid_re.append(
                jnp.concatenate([2.0 * t for t in top_re[half:]] + [zero] * half, 1)
            )
            mid_im.append(
                jnp.concatenate([2.0 * t for t in top_im[half:]] + [zero] * half, 1)
            )
            f_re = jnp.where(
                first, jnp.concatenate(base_re, 1), jnp.concatenate(f_re, 1)
            )
            f_im = jnp.where(
                first, jnp.concatenate(base_im, 1), jnp.concatenate(f_im, 1)
            )
            x_re = bins[rows, :seq_len]
            x_im = bins[rows, seq_len:]
            stack[rows, :seq_len] = f_re * x_re - f_im * x_im
            stack[rows, seq_len:] = -(f_re * x_im + f_im * x_re)
        pad = jnp.zeros((half_rows - 2 * slots - 2, seq_len), F32)
        f_re = jnp.concatenate([*mid_re, pad], 0)
        f_im = jnp.concatenate([*mid_im, pad], 0)
        rows = pl.ds(base + 2 * slots, half_rows - 2 * slots)
        x_re = bins[rows, :seq_len]
        x_im = bins[rows, seq_len:]
        stack[rows, :seq_len] = f_re * x_re - f_im * x_im
        stack[rows, seq_len:] = -(f_re * x_im + f_im * x_re)

        group = pl.ds(base, half_rows)
        back = dft_dot(stack[group, :], dft)
        tail = back[2 * slots :]
        tail = tail[:, :seq_len] * middle[0:1] + tail[:, seq_len:] * middle[1:2]
        for h in range(2):
            part = back[h * slots : (h + 1) * slots]
            re = part[:, :seq_len]
            im = part[:, seq_len:]
            cos_t = twiddle[0]
            sin_t = twiddle[1]
            v_re = re * cos_t + im * sin_t
            v_im = jnp.where(first, tail[h : h + 1], im * cos_t - re * sin_t)
            conv = table_dot(inv, jnp.concatenate([v_re, v_im], 0))
            for mt in range(m_tiles):
                send_y[g, pl.ds(h * m_tiles + mt, blocks, stride=f_rows), :] = conv[
                    :, mt * LANES : (mt + 1) * LANES
                ]
        exchange(send_y.at[g], recv_y.at[g], f_rows, y_sem.at[g])

    for g in range(2):
        wait_all(recv_y.at[g], f_rows, y_sem.at[g, 1])
        for h in range(2):
            ct = 2 * h + g
            for mt in range(m_tiles):
                tile = recv_y[g, pl.ds(h * m_tiles + mt, blocks, stride=f_rows), :]
                out_ref[
                    mt * LANES : (mt + 1) * LANES, ct * LANES : (ct + 1) * LANES
                ] = tile.T

    wait_all(send_x, x_rows, x_sem.at[0])
    for g in range(2):
        wait_all(send_f.at[g], f_rows, f_sem.at[g, 0])
        wait_all(send_y.at[g], f_rows, y_sem.at[g, 0])


def body(signal, spectrum, skip_gain):
    blocks = lax.axis_size(("outer", "inner"))
    inner = lax.axis_size("inner")
    seq_len, channels = signal.shape
    fwd, inv, dft, twiddle, middle = tables(blocks, seq_len)
    chan_tiles = channels // LANES
    m_tiles = seq_len // LANES
    x_rows = chan_tiles * m_tiles
    f_rows = 2 * m_tiles
    stack_rows = 2 * (blocks + 16)
    vmem = pltpu.VMEM
    dma = pltpu.SemaphoreType.DMA
    any_spec = pl.BlockSpec(memory_space=pl.ANY)
    conv = pl.pallas_call(
        functools.partial(kernel, blocks, inner),
        out_shape=jax.ShapeDtypeStruct(signal.shape, F32),
        in_specs=[any_spec] * 7,
        out_specs=pl.BlockSpec(memory_space=pltpu.VMEM),
        scratch_shapes=[
            vmem(signal.shape, F32),
            vmem(spectrum.shape[1:], F32),
            vmem(dft.shape, BF16),
            vmem(fwd.shape, BF16),
            vmem(inv.shape, BF16),
            vmem(twiddle.shape, F32),
            vmem(middle.shape, F32),
            vmem((blocks * x_rows, LANES), F32),
            vmem((blocks * x_rows, LANES), F32),
            vmem((2, blocks * f_rows, LANES), F32),
            vmem((2, blocks * f_rows, LANES), F32),
            vmem((2, blocks * f_rows, LANES), F32),
            vmem((2, blocks * f_rows, LANES), F32),
            vmem((stack_rows, 2 * seq_len), F32),
            vmem((stack_rows, 2 * seq_len), F32),
            dma((7,)),
            dma((2,)),
            dma((2, 2)),
            dma((2, 2)),
        ],
        compiler_params=pltpu.CompilerParams(
            collective_id=1, has_side_effects=True, vmem_limit_bytes=48 * 2**20
        ),
        cost_estimate=pl.CostEstimate(
            flops=5 * 10**9, bytes_accessed=8 * 2**20, transcendentals=0
        ),
        name="hyena_conv",
    )(
        signal,
        spectrum.reshape(spectrum.shape[1:]),
        dft,
        fwd,
        inv,
        twiddle,
        middle,
    )
    return conv + skip_gain[None, :] * signal


def solution(mesh):
    return jax.shard_map(
        body,
        mesh=mesh,
        in_specs=(P(("outer", "inner"), None), P(("outer", "inner"), None, None, None), P()),
        out_specs=P(("outer", "inner"), None),
        check_vma=False,
    )
```

profile of v0, /device:TPU:1, one launch (start us, length us, event | category | flops | bytes accessed | tf_op | source)
XLA Modules:
  0.0 59.7 jit_solution(15952939294209936124)
XLA Ops:
  0.0 0.0 copy-start
  0.0 1.2 %copy-done = f32[512,512]{1,0:T(8,128)S(1)} copy-done((f32[512,512]{1,0:T(8,128)S(1)}, f32[512,512]{1,0:T(8,128)}, u32[]{:S(2)}) %copy-start) | copy-done | bytes 1048600
  1.2 0.0 copy-start.1
  1.2 1.2 %copy-done.1 = f32[1,2,512,256]{3,2,1,0:T(8,128)S(1)} copy-done((f32[1,2,512,256]{3,2,1,0:T(8,128)S(1)}, f32[1,2,512,256]{3,2,1,0:T(8,128)}, u32[]{:S(2)}) %copy-start.1) | copy-done | bytes 1048600
  2.5 0.0 copy-start.2
  2.5 0.9 %copy-done.2 = f32[2,64,512]{2,1,0:T(8,128)S(1)} copy-done((f32[2,64,512]{2,1,0:T(8,128)S(1)}, f32[2,64,512]{2,1,0:T(8,128)}, u32[]{:S(2)}) %copy-start.2) | copy-done | bytes 262168
  3.4 0.0 copy-start.3
  3.4 0.8 %copy-done.3 = bf16[2,128,128]{2,1,0:T(8,128)(2,1)S(1)} copy-done((bf16[2,128,128]{2,1,0:T(8,128)(2,1)S(1)}, bf16[2,128,128]{2,1,0:T(8,128)(2,1)}, u32[]{:S(2)}) %copy-start.3) | copy-done | bytes 65560
  4.2 0.0 copy-start.4
  4.2 0.8 %copy-done.4 = bf16[2,128,128]{2,1,0:T(8,128)(2,1)S(1)} copy-done((bf16[2,128,128]{2,1,0:T(8,128)(2,1)S(1)}, bf16[2,128,128]{2,1,0:T(8,128)(2,1)}, u32[]{:S(2)}) %copy-start.4) | copy-done | bytes 65560
  5.1 0.0 copy-start.5
  5.1 0.7 %copy-done.5 = f32[8,512]{1,0:T(8,128)S(1)} copy-done((f32[8,512]{1,0:T(8,128)S(1)}, f32[8,512]{1,0:T(8,128)}, u32[]{:S(2)}) %copy-start.5) | copy-done | bytes 16408
  5.8 0.0 copy-start.6
  5.8 52.7 %hyena_conv.1 = f32[512,512]{1,0:T(8,128)S(1)} custom-call(f32[512,512]{1,0:T(8,128)S(1)} %copy-done, f32[2,512,256]{2,1,0:T(8,128)S(1)} %bitcast.1, bf16[2,1024,1024]{2,1,0:T(8,128)(2,1)} %constant.10.clone.dft_hbm, bf16[2,128,128]{2,1,0:T(8,128)(2,1)S(1)} %copy-done.4, bf16[2,128,128]{2,1,0:T(8,128)(2,1)S(1)} %copy-done.3, f32[2,64,512]{2,1,0:T(8,128)S(1)} %copy-done.2, ...), custom_call_target="tpu_custom_call" | custom-call | flops 5000000000 | bytes 8388608 | tf_op jit(solution)/shard_map/hyena_conv/pallas_call | solution.py:313
  58.5 0.0 copy-done.6
  58.5 1.2 %multiply_add_fusion = f32[512,512]{1,0:T(8,128)} fusion(f32[512,512]{1,0:T(8,128)S(1)} %hyena_conv.1, f32[512,512]{1,0:T(8,128)S(1)} %copy-done, f32[512]{0:T(512)S(1)} %copy-done.6), kind=kLoop, calls=%fused_computation | loop fusion | flops 524288 | bytes 3147776 | tf_op jit(solution)/shard_map/add | solution.py:355
Async XLA Ops:
  0.0 1.2 %copy-start = (f32[512,512]{1,0:T(8,128)S(1)}, f32[512,512]{1,0:T(8,128)}, u32[]{:S(2)}) copy-start(f32[512,512]{1,0:T(8,128)} %signal_hbm.1) | copy-start | bytes 3145732
  1.2 1.2 %copy-start.1 = (f32[1,2,512,256]{3,2,1,0:T(8,128)S(1)}, f32[1,2,512,256]{3,2,1,0:T(8,128)}, u32[]{:S(2)}) copy-start(f32[1,2,512,256]{3,2,1,0:T(8,128)} %param.9) | copy-start | bytes 3145732
  2.5 0.9 %copy-start.2 = (f32[2,64,512]{2,1,0:T(8,128)S(1)}, f32[2,64,512]{2,1,0:T(8,128)}, u32[]{:S(2)}) copy-start(f32[2,64,512]{2,1,0:T(8,128)} %constant.13.clone.twiddle_hbm) | copy-start | bytes 786436
  3.4 0.8 %copy-start.3 = (bf16[2,128,128]{2,1,0:T(8,128)(2,1)S(1)}, bf16[2,128,128]{2,1,0:T(8,128)(2,1)}, u32[]{:S(2)}) copy-start(bf16[2,128,128]{2,1,0:T(8,128)(2,1)} %constant.12.clone.inv_hbm) | copy-start | bytes 196612
  4.2 0.8 %copy-start.4 = (bf16[2,128,128]{2,1,0:T(8,128)(2,1)S(1)}, bf16[2,128,128]{2,1,0:T(8,128)(2,1)}, u32[]{:S(2)}) copy-start(bf16[2,128,128]{2,1,0:T(8,128)(2,1)} %constant.11.clone.fwd_hbm) | copy-start | bytes 196612
  5.1 0.7 %copy-start.5 = (f32[8,512]{1,0:T(8,128)S(1)}, f32[8,512]{1,0:T(8,128)}, u32[]{:S(2)}) copy-start(f32[8,512]{1,0:T(8,128)} %constant.14.clone.middle_hbm) | copy-start | bytes 49156
  5.8 52.7 %copy-start.6 = (f32[512]{0:T(512)S(1)}, f32[512]{0:T(512)}, u32[]{:S(2)}) copy-start(f32[512]{0:T(512)} %param.10) | copy-start | bytes 6148
where the time goes:
time: 60.1 us; the launch traced here: 59.7 us
  Pallas kernels  52.7 us (88%)
  local copies, waits for them, and re-layouts  5.8 us (10%)
  other arithmetic  1.2 us (2%)
    pallas_call x1, Pallas kernels, body(): pl.pallas_call(functools.partial(kernel, blocks, inner), out_shape=jax.Sh...  52.7 us
    unnamed x14, local copies, waits for them, and re-layouts  5.8 us

commit v1 on v0

v1 whole, which is shorter than its diff:
```python
import functools
import itertools
import math
import random

import jax
import jax.numpy as jnp
import ml_dtypes
import numpy as np
from jax import lax
from jax.experimental import pallas as pl
from jax.experimental.pallas import tpu as pltpu
from jax.sharding import PartitionSpec as P

F32 = jnp.float32
BF16 = jnp.bfloat16
LANES = 128


def halves(table):
    high = table.astype(ml_dtypes.bfloat16)
    low = (table - high.astype(np.float64)).astype(ml_dtypes.bfloat16)
    return high, low


def tables(blocks, seq_len):
    slots = blocks // 2
    total = blocks * seq_len
    d = np.arange(blocks)
    s = np.arange(slots)
    m = np.arange(seq_len)
    angle = 2.0 * math.pi / blocks * (s[:, None] * d[None, :] % blocks)
    cos_rows = np.cos(angle)
    sin_rows = np.sin(angle)
    sin_rows[0] = np.where(d % 2 == 0, -1.0, 1.0)
    fwd = np.concatenate([cos_rows, -sin_rows], 0)
    scale = np.where(s == 0, 1.0, 2.0)[:, None] / total
    minus = sin_rows * scale
    minus[0] = np.where(d % 2 == 0, 1.0, -1.0) * scale[0]
    inv = np.concatenate([cos_rows * scale, minus], 0).T
    turn = 2.0 * math.pi / total * (np.arange(slots + 1)[:, None] * m[None, :] % total)
    twiddle = np.stack([np.cos(turn[:slots]), np.sin(turn[:slots])]).astype(np.float32)
    middle = np.stack([np.cos(turn[slots]), np.sin(turn[slots])]).astype(np.float32)
    middle = np.concatenate([middle, np.zeros((6, seq_len), np.float32)], 0)
    theta = 2.0 * math.pi / seq_len * (m[:, None] * m[None, :] % seq_len)
    cos_t = np.cos(theta)
    sin_t = np.sin(theta)
    dft = np.concatenate(
        [np.concatenate([cos_t, -sin_t], 1), np.concatenate([sin_t, cos_t], 1)], 0
    )
    fwd_hl = np.stack(halves(fwd))
    inv_hl = np.stack(halves(inv))
    dft_hl = np.stack(halves(dft))
    return fwd_hl, inv_hl, dft_hl, twiddle, middle


def split(value):
    high = value.astype(BF16)
    return high, (value - high.astype(F32)).astype(BF16)


def mm(left, right):
    return jnp.dot(left, right, preferred_element_type=F32)


def table_dot(table_ref, value):
    high, low = split(value)
    return mm(table_ref[0], high) + mm(table_ref[0], low) + mm(table_ref[1], high)


def dft_dot(rows, dft_ref):
    high, low = split(rows)
    return mm(high, dft_ref[0]) + mm(low, dft_ref[0]) + mm(high, dft_ref[1])


def offsets(mesh_shape):
    axes = [range(n) for n in mesh_shape]
    every = [o for o in itertools.product(*axes) if any(o)]

    def hops(o):
        z, _, x, y = [min(d, n - d) for d, n in zip(o, mesh_shape)]
        return z + x + y

    random.Random(1).shuffle(every)
    return sorted(every, key=lambda o: -hops(o))


def kernel(
    shape,
    signal_hbm,
    spectrum_hbm,
    dft_hbm,
    fwd_hbm,
    inv_hbm,
    twiddle_hbm,
    middle_hbm,
    out_ref,
    signal,
    spectrum,
    dft,
    fwd,
    inv,
    twiddle,
    middle,
    send_x,
    recv_x,
    send_f,
    recv_f,
    send_y,
    recv_y,
    stack,
    bins,
    load_sem,
    x_sem,
    f_sem,
    y_sem,
):
    n_z, n_core, n_x, n_y = shape
    outer = lax.axis_index("outer")
    inner = lax.axis_index("inner")
    n_outer = n_z * n_core
    n_inner = n_x * n_y
    blocks = n_outer * n_inner
    me = outer * n_inner + inner
    slots = blocks // 2
    seq_len = signal.shape[0]
    m_tiles = seq_len // LANES
    rows = 2 * m_tiles
    stack_rows = stack.shape[1]

    def lanes(tile):
        return pl.ds(tile * LANES, LANES)

    loads = {}

    def load(name, src, dst):
        copy = pltpu.make_async_copy(src, dst, load_sem.at[len(loads)])
        copy.start()
        loads[name] = copy

    for g in range(2):
        for h in range(2):
            where = lanes(2 * h + g)
            load(("x", g, h), signal_hbm.at[:, where], signal.at[:, where])

    barrier = pltpu.get_barrier_semaphore()

    @pl.loop(0, n_outer)
    def _(o):
        for i in range(n_inner):

            @pl.when(jnp.logical_or(o != outer, inner != i))
            def _():
                pl.semaphore_signal(
                    barrier,
                    inc=1,
                    device_id=(o, i),
                    device_id_type=pl.DeviceIdType.MESH,
                )

    for g in range(2):
        load(("f", g), spectrum_hbm.at[:, :, lanes(g)], spectrum.at[:, :, lanes(g)])
    load("fwd", fwd_hbm, fwd)
    load("twiddle", twiddle_hbm, twiddle)
    load("middle", middle_hbm, middle)
    load("dft", dft_hbm, dft)
    load("inv", inv_hbm, inv)

    z, core = outer // n_core, lax.rem(outer, n_core)
    x, y = inner // n_y, lax.rem(inner, n_y)
    at_outer = [
        [lax.rem(z + d, n_z) * n_core + lax.rem(core + e, n_core) for e in range(n_core)]
        for d in range(n_z)
    ]
    at_x = [lax.rem(x + d, n_x) * n_y for d in range(n_x)]
    at_y = [lax.rem(y + d, n_y) for d in range(n_y)]
    order = offsets(shape)

    def block(ref, index):
        return ref.at[pl.ds(pl.multiple_of(index * rows, rows), rows)]

    def exchange(src, dst, sems):
        for dz, dc, dx, dy in order:
            to = (at_outer[dz][dc], at_x[dx] + at_y[dy])
            pltpu.make_async_remote_copy(
                src_ref=block(src, to[0] * n_inner + to[1]),
                dst_ref=block(dst, me),
                send_sem=sems.at[0],
                recv_sem=sems.at[1],
                device_id=to,
                device_id_type=pl.DeviceIdType.MESH,
            ).start()
        own = pl.ds(pl.multiple_of(me * rows, rows), rows)
        dst[own, :] = src[own, :]

    def wait_all(ref, sem):
        part = ref.at[pl.ds(0, (blocks - 1) * rows)]
        pltpu.make_async_copy(part, part, sem).wait()

    def spread(ref, g, index, tile):
        ref[g, pl.ds(index, blocks, stride=rows), :] = tile

    for g in range(2):
        for h in range(2):
            loads["x", g, h].wait()
            for mt in range(m_tiles):
                spread(send_x, g, h * m_tiles + mt, signal[lanes(mt), lanes(2 * h + g)].T)
        if g == 0:
            pl.semaphore_wait(barrier, blocks - 1)
        exchange(send_x.at[g], recv_x.at[g], x_sem.at[g])
        loads["f", g].wait()
        for r in range(2):
            for bt in range(m_tiles):
                spread(send_f, g, r * m_tiles + bt, spectrum[r, lanes(bt), lanes(g)].T)
        exchange(send_f.at[g], recv_f.at[g], f_sem.at[g])

    for name in ("fwd", "twiddle", "middle", "dft", "inv"):
        loads[name].wait()
    first = lax.broadcasted_iota(jnp.int32, (slots, seq_len), 0) == 0
    lane = lax.broadcasted_iota(jnp.int32, (1, LANES), 1)
    last_rows = pl.ds(2 * slots, stack_rows - 2 * slots)
    pad = jnp.zeros((stack_rows - 2 * slots - 2, seq_len), F32)

    def forward(g):
        extra = []
        for h in range(2):
            data = jnp.concatenate(
                [
                    recv_x[g, pl.ds(h * m_tiles + mt, blocks, stride=rows), :]
                    for mt in range(m_tiles)
                ],
                1,
            )
            packed = table_dot(fwd, data)
            re = packed[:slots]
            im = packed[slots:]
            cos_t = twiddle[0]
            sin_t = twiddle[1]
            at = pl.ds(h * slots, slots)
            stack[g, at, :seq_len] = re * cos_t + im * sin_t
            stack[g, at, seq_len:] = jnp.where(first, 0.0, im * cos_t - re * sin_t)
            extra.append(im[0:1])
        middle_in = jnp.concatenate([*extra, pad], 0)
        stack[g, last_rows, :seq_len] = middle_in * middle[0:1]
        stack[g, last_rows, seq_len:] = -middle_in * middle[1:2]
        bins[g] = dft_dot(stack[g], dft)

    def times_filter(g, at, f_re, f_im):
        x_re = bins[g, at, :seq_len]
        x_im = bins[g, at, seq_len:]
        stack[g, at, :seq_len] = f_re * x_re - f_im * x_im
        stack[g, at, seq_len:] = -(f_re * x_im + f_im * x_re)

    def backward(g):
        mid_re = []
        mid_im = []
        for h in range(2):
            f_re, f_im = [
                [
                    recv_f[
                        g, pl.ds((h * 2 + r) * m_tiles + bt, slots, stride=2 * rows), :
                    ]
                    for bt in range(m_tiles)
                ]
                for r in range(2)
            ]
            top_re = [t[0:1] for t in f_re]
            top_im = [t[0:1] for t in f_im]
            half = m_tiles // 2
            zero = jnp.zeros((1, LANES), F32)
            base_re = [2.0 * t for t in top_re[:half]] + [zero] * half
            base_im = [2.0 * t for t in top_im[:half]] + [zero] * half
            base_re[0] = jnp.where(lane == 0, top_re[0], base_re[0])
            base_im[0] = jnp.where(lane == 0, 0.0, base_im[0])
            base_re[half] = jnp.where(lane == 0, top_im[0], 0.0)
            mid_re.append(
                jnp.concatenate([2.0 * t for t in top_re[half:]] + [zero] * half, 1)
            )
            mid_im.append(
                jnp.concatenate([2.0 * t for t in top_im[half:]] + [zero] * half, 1)
            )
            times_filter(
                g,
                pl.ds(h * slots, slots),
                jnp.where(first, jnp.concatenate(base_re, 1), jnp.concatenate(f_re, 1)),
                jnp.where(first, jnp.concatenate(base_im, 1), jnp.concatenate(f_im, 1)),
            )
        times_filter(
            g,
            last_rows,
            jnp.concatenate([*mid_re, pad], 0),
            jnp.concatenate([*mid_im, pad], 0),
        )
        back = dft_dot(stack[g], dft)
        tail = back[2 * slots :]
        tail = tail[:, :seq_len] * middle[0:1] + tail[:, seq_len:] * middle[1:2]
        for h in range(2):
            part = back[h * slots : (h + 1) * slots]
            re = part[:, :seq_len]
            im = part[:, seq_len:]
            cos_t = twiddle[0]
            sin_t = twiddle[1]
            v_re = re * cos_t + im * sin_t
            v_im = jnp.where(first, tail[h : h + 1], im * cos_t - re * sin_t)
            conv = table_dot(inv, jnp.concatenate([v_re, v_im], 0))
            for mt in range(m_tiles):
                spread(send_y, g, h * m_tiles + mt, conv[:, mt * LANES : (mt + 1) * LANES])

    for g in range(2):
        wait_all(recv_x.at[g], x_sem.at[g, 1])
        forward(g)
        wait_all(recv_f.at[g], f_sem.at[g, 1])
        backward(g)
        exchange(send_y.at[g], recv_y.at[g], y_sem.at[g])

    for g in range(2):
        wait_all(recv_y.at[g], y_sem.at[g, 1])
        for h in range(2):
            for mt in range(m_tiles):
                tile = recv_y[g, pl.ds(h * m_tiles + mt, blocks, stride=rows), :]
                out_ref[lanes(mt), lanes(2 * h + g)] = tile.T

    for g in range(2):
        wait_all(send_x.at[g], x_sem.at[g, 0])
        wait_all(send_f.at[g], f_sem.at[g, 0])
        wait_all(send_y.at[g], y_sem.at[g, 0])


def body(signal, spectrum, skip_gain):
    n_outer = lax.axis_size("outer")
    n_inner = lax.axis_size("inner")
    blocks = n_outer * n_inner
    side = math.isqrt(n_inner)
    shape = (n_outer // 2, 2, side, side)
    seq_len, channels = signal.shape
    fwd, inv, dft, twiddle, middle = tables(blocks, seq_len)
    rows = 2 * (seq_len // LANES)
    vmem = pltpu.VMEM
    dma = pltpu.SemaphoreType.DMA
    in_hbm = pl.BlockSpec(memory_space=pltpu.HBM)
    conv = pl.pallas_call(
        functools.partial(kernel, shape),
        out_shape=jax.ShapeDtypeStruct(signal.shape, F32),
        in_specs=[in_hbm] * 7,
        out_specs=pl.BlockSpec(memory_space=pltpu.VMEM),
        scratch_shapes=[
            vmem(signal.shape, F32),
            vmem(spectrum.shape[1:], F32),
            vmem(dft.shape, BF16),
            vmem(fwd.shape, BF16),
            vmem(inv.shape, BF16),
            vmem(twiddle.shape, F32),
            vmem(middle.shape, F32),
            *[vmem((2, blocks * rows, LANES), F32) for _ in range(6)],
            *[vmem((2, blocks + 16, 2 * seq_len), F32) for _ in range(2)],
            dma((11,)),
            *[dma((2, 2)) for _ in range(3)],
        ],
        compiler_params=pltpu.CompilerParams(
            collective_id=1, has_side_effects=True, vmem_limit_bytes=48 * 2**20
        ),
        cost_estimate=pl.CostEstimate(
            flops=5 * 10**9, bytes_accessed=8 * 2**20, transcendentals=0
        ),
        name="hyena_conv",
    )(
        *[
            pltpu.with_memory_space_constraint(a, pltpu.HBM)
            for a in (
                signal,
                spectrum.reshape(spectrum.shape[1:]),
                dft,
                fwd,
                inv,
                twiddle,
                middle,
            )
        ]
    )
    return conv + skip_gain[None, :] * signal


def solution(mesh):
    return jax.shard_map(
        body,
        mesh=mesh,
        in_specs=(P(("outer", "inner"), None), P(("outer", "inner"), None, None, None), P()),
        out_specs=P(("outer", "inner"), None),
        check_vma=False,
    )
```

time: 60.1 us -> 49.5 us (0.82)
  local copies, waits for them, and re-layouts: 5.8 us -> 0.01 us
  Pallas kernels: 52.7 us -> 48.2 us
    unnamed x14 -> x4, local copies, waits for them, and re-layouts: 5.8 us -> 0.01 us
    pallas_call x1, Pallas kernels: 52.7 us -> 48.2 us  [body(): pl.pallas_call(functools.partial(kernel, shape), out_shape=jax.ShapeDtype...]
where the time goes in v1:
time: 49.5 us; the launch traced here: 49.4 us
  Pallas kernels  48.2 us (97%)
  other arithmetic  1.2 us (2%)
    pallas_call x1, Pallas kernels, body(): pl.pallas_call(functools.partial(kernel, shape), out_shape=jax.ShapeDtype...  48.2 us
    add x1, other arithmetic, body(): return conv + skip_gain[None, :] * signal  1.2 us

profile of v1, /device:TPU:1, one launch (start us, length us, event | category | flops | bytes accessed | tf_op | source)
XLA Modules:
  0.0 49.4 jit_solution(8414487153274688798)
XLA Ops:
  0.0 0.0 copy-start
  0.0 0.0 copy-start.1
  0.0 48.2 %hyena_conv.1 = f32[512,512]{1,0:T(8,128)S(1)} custom-call(f32[512,512]{1,0:T(8,128)} %signal_hbm.1, f32[2,512,256]{2,1,0:T(8,128)} %bitcast.1, bf16[2,1024,1024]{2,1,0:T(8,128)(2,1)} %constant.10.clone.dft_hbm, bf16[2,128,128]{2,1,0:T(8,128)(2,1)} %constant.11.clone.fwd_hbm, bf16[2,128,128]{2,1,0:T(8,128)(2,1)} %constant.12.clone.inv_hbm, ...), custom_call_target="tpu_custom_call" | custom-call | flops 5000000000 | bytes 8388608 | tf_op jit(solution)/shard_map/hyena_conv/pallas_call | solution.py:341
  48.2 0.0 copy-done
  48.2 0.0 copy-done.1
  48.2 1.2 %multiply_add_fusion = f32[512,512]{1,0:T(8,128)} fusion(f32[512,512]{1,0:T(8,128)S(1)} %hyena_conv.1, f32[512,512]{1,0:T(8,128)S(1)} %copy-done, f32[512]{0:T(512)S(1)} %copy-done.1), kind=kLoop, calls=%fused_computation | loop fusion | flops 524288 | bytes 3147776 | tf_op jit(solution)/shard_map/add | solution.py:380
Async XLA Ops:
  0.0 48.2 %copy-start = (f32[512,512]{1,0:T(8,128)S(1)}, f32[512,512]{1,0:T(8,128)}, u32[]{:S(2)}) copy-start(f32[512,512]{1,0:T(8,128)} %signal_hbm.1) | copy-start | bytes 3145732
  0.0 48.2 %copy-start.1 = (f32[512]{0:T(512)S(1)}, f32[512]{0:T(512)}, u32[]{:S(2)}) copy-start(f32[512]{0:T(512)} %param.10) | copy-start | bytes 6148

commit v2 on v1

--- a/solution.py
+++ b/solution.py
@@ -15,6 +15,7 @@
 F32 = jnp.float32
 BF16 = jnp.bfloat16
 LANES = 128
+RADIX = 4
 
 
 def halves(table):
@@ -35,22 +36,24 @@
     sin_rows[0] = np.where(d % 2 == 0, -1.0, 1.0)
     fwd = np.concatenate([cos_rows, -sin_rows], 0)
     scale = np.where(s == 0, 1.0, 2.0)[:, None] / total
-    minus = sin_rows * scale
-    minus[0] = np.where(d % 2 == 0, 1.0, -1.0) * scale[0]
-    inv = np.concatenate([cos_rows * scale, minus], 0).T
+    inv = (fwd * np.concatenate([scale, scale], 0)).T
     turn = 2.0 * math.pi / total * (np.arange(slots + 1)[:, None] * m[None, :] % total)
     twiddle = np.stack([np.cos(turn[:slots]), np.sin(turn[:slots])]).astype(np.float32)
     middle = np.stack([np.cos(turn[slots]), np.sin(turn[slots])]).astype(np.float32)
     middle = np.concatenate([middle, np.zeros((6, seq_len), np.float32)], 0)
-    theta = 2.0 * math.pi / seq_len * (m[:, None] * m[None, :] % seq_len)
+    n = np.arange(LANES)[None, :, None]
+    l = np.arange(LANES)[None, None, :]
+    r = np.arange(RADIX)[:, None, None]
+    theta = 2.0 * math.pi / seq_len * (n * (r + RADIX * l) % seq_len)
     cos_t = np.cos(theta)
     sin_t = np.sin(theta)
     dft = np.concatenate(
-        [np.concatenate([cos_t, -sin_t], 1), np.concatenate([sin_t, cos_t], 1)], 0
+        [np.concatenate([cos_t, -sin_t], 2), np.concatenate([sin_t, cos_t], 2)], 1
     )
+    dft = np.stack([dft, dft.transpose(0, 2, 1)])
     fwd_hl = np.stack(halves(fwd))
     inv_hl = np.stack(halves(inv))
-    dft_hl = np.stack(halves(dft))
+    dft_hl = np.stack(halves(dft), 1)
     return fwd_hl, inv_hl, dft_hl, twiddle, middle
 
 
@@ -68,9 +71,15 @@
     return mm(table_ref[0], high) + mm(table_ref[0], low) + mm(table_ref[1], high)
 
 
-def dft_dot(rows, dft_ref):
-    high, low = split(rows)
-    return mm(high, dft_ref[0]) + mm(low, dft_ref[0]) + mm(high, dft_ref[1])
+def radix4(parts, direction):
+    (ar, ai), (br, bi), (cr, ci), (dr, di) = parts
+    pr, pi, qr, qi = ar + cr, ai + ci, ar - cr, ai - ci
+    sr, si, tr, ti = br + dr, bi + di, br - dr, bi - di
+    plus = (qr - ti, qi + tr)
+    minus = (qr + ti, qi - tr)
+    if direction < 0:
+        plus, minus = minus, plus
+    return (pr + sr, pi + si), plus, (pr - sr, pi - si), minus
 
 
 def offsets(mesh_shape):
@@ -82,7 +91,7 @@
         return z + x + y
 
     random.Random(1).shuffle(every)
-    return sorted(every, key=lambda o: -hops(o))
+    return every, sorted(every, key=lambda o: -hops(o))
 
 
 def kernel(
@@ -108,8 +117,9 @@
     recv_f,
     send_y,
     recv_y,
-    stack,
+    parts,
     bins,
+    back,
     load_sem,
     x_sem,
     f_sem,
@@ -126,7 +136,7 @@
     seq_len = signal.shape[0]
     m_tiles = seq_len // LANES
     rows = 2 * m_tiles
-    stack_rows = stack.shape[1]
+    lines = bins.shape[2]
 
     def lanes(tile):
         return pl.ds(tile * LANES, LANES)
@@ -159,7 +169,7 @@
                 )
 
     for g in range(2):
-        load(("f", g), spectrum_hbm.at[:, :, lanes(g)], spectrum.at[:, :, lanes(g)])
+        load(("f", g), spectrum_hbm.at[:, :, lanes(g)], spectrum.at[g])
     load("fwd", fwd_hbm, fwd)
     load("twiddle", twiddle_hbm, twiddle)
     load("middle", middle_hbm, middle)
@@ -174,12 +184,12 @@
     ]
     at_x = [lax.rem(x + d, n_x) * n_y for d in range(n_x)]
     at_y = [lax.rem(y + d, n_y) for d in range(n_y)]
-    order = offsets(shape)
+    mixed, far = offsets(shape)
 
     def block(ref, index):
         return ref.at[pl.ds(pl.multiple_of(index * rows, rows), rows)]
 
-    def exchange(src, dst, sems):
+    def exchange(src, dst, sems, order):
         for dz, dc, dx, dy in order:
             to = (at_outer[dz][dc], at_x[dx] + at_y[dy])
             pltpu.make_async_remote_copy(
@@ -207,22 +217,40 @@
                 spread(send_x, g, h * m_tiles + mt, signal[lanes(mt), lanes(2 * h + g)].T)
         if g == 0:
             pl.semaphore_wait(barrier, blocks - 1)
-        exchange(send_x.at[g], recv_x.at[g], x_sem.at[g])
+        exchange(send_x.at[g], recv_x.at[g], x_sem.at[g], mixed)
         loads["f", g].wait()
         for r in range(2):
-            for bt in range(m_tiles):
-                spread(send_f, g, r * m_tiles + bt, spectrum[r, lanes(bt), lanes(g)].T)
-        exchange(send_f.at[g], recv_f.at[g], f_sem.at[g])
+            for q in range(RADIX):
+                every = pl.ds(q, LANES, stride=RADIX)
+                spread(send_f, g, r * m_tiles + q, spectrum[g, r, every, :].T)
+        exchange(send_f.at[g], recv_f.at[g], f_sem.at[g], (mixed, far)[g])
 
     for name in ("fwd", "twiddle", "middle", "dft", "inv"):
         loads[name].wait()
-    first = lax.broadcasted_iota(jnp.int32, (slots, seq_len), 0) == 0
+    first = lax.broadcasted_iota(jnp.int32, (slots, LANES), 0) == 0
     lane = lax.broadcasted_iota(jnp.int32, (1, LANES), 1)
-    last_rows = pl.ds(2 * slots, stack_rows - 2 * slots)
-    pad = jnp.zeros((stack_rows - 2 * slots - 2, seq_len), F32)
+    extra_rows = lines - 2 * slots
+    pad = jnp.zeros((extra_rows - 2, LANES), F32)
+    tiles = [slice(p * LANES, (p + 1) * LANES) for p in range(RADIX)]
+
+    def put(p, at, count, re, im):
+        value = jnp.concatenate([re, im], 1)
+        high, low = split(value)
+        parts[p, pl.ds(at, count), :] = high
+        parts[p, pl.ds(lines + at, count), :] = low
+
+    def transform(p, way):
+        whole = mm(parts[p], dft[way, 0, p])
+        rest = mm(parts[p, :lines], dft[way, 1, p])
+        return whole[:lines] + whole[lines:] + rest
 
     def forward(g):
         extra = []
+
+        def lines_in(at, count, pairs):
+            for p, (re, im) in enumerate(radix4(pairs, -1)):
+                put(p, at, count, re, im)
+
         for h in range(2):
             data = jnp.concatenate(
                 [
@@ -232,86 +260,110 @@
                 1,
             )
             packed = table_dot(fwd, data)
-            re = packed[:slots]
-            im = packed[slots:]
-            cos_t = twiddle[0]
-            sin_t = twiddle[1]
-            at = pl.ds(h * slots, slots)
-            stack[g, at, :seq_len] = re * cos_t + im * sin_t
-            stack[g, at, seq_len:] = jnp.where(first, 0.0, im * cos_t - re * sin_t)
-            extra.append(im[0:1])
-        middle_in = jnp.concatenate([*extra, pad], 0)
-        stack[g, last_rows, :seq_len] = middle_in * middle[0:1]
-        stack[g, last_rows, seq_len:] = -middle_in * middle[1:2]
-        bins[g] = dft_dot(stack[g], dft)
-
-    def times_filter(g, at, f_re, f_im):
-        x_re = bins[g, at, :seq_len]
-        x_im = bins[g, at, seq_len:]
-        stack[g, at, :seq_len] = f_re * x_re - f_im * x_im
-        stack[g, at, seq_len:] = -(f_re * x_im + f_im * x_re)
+            extra.append(packed[slots : slots + 1])
+            pairs = []
+            for t in tiles:
+                re = packed[:slots, t]
+                im = packed[slots:, t]
+                cos_t = twiddle[0, :, t]
+                sin_t = twiddle[1, :, t]
+                pairs.append(
+                    (
+                        re * cos_t + im * sin_t,
+                        jnp.where(first, 0.0, im * cos_t - re * sin_t),
+                    )
+                )
+            lines_in(h * slots, slots, pairs)
+        pairs = []
+        for t in tiles:
+            value = jnp.concatenate([extra[0][:, t], extra[1][:, t], pad], 0)
+            pairs.append((value * middle[0:1, t], -value * middle[1:2, t]))
+        lines_in(2 * slots, extra_rows, pairs)
+        for p in range(RADIX):
+            bins[g, p] = transform(p, 0)
+
+    def times_filter(g, p, at, count, f_re, f_im):
+        x_re = bins[g, p, pl.ds(at, count), :LANES]
+        x_im = bins[g, p, pl.ds(at, count), LANES:]
+        put(p, at, count, f_re * x_re - f_im * x_im, f_re * x_im + f_im * x_re)
 
     def backward(g):
-        mid_re = []
-        mid_im = []
-        for h in range(2):
-            f_re, f_im = [
-                [
+        lower = lane < LANES // 2
+        for p in range(RADIX):
+            mid = []
+            for h in range(2):
+                f_re, f_im = [
                     recv_f[
-                        g, pl.ds((h * 2 + r) * m_tiles + bt, slots, stride=2 * rows), :
+                        g, pl.ds((h * 2 + r) * m_tiles + p, slots, stride=2 * rows), :
                     ]
-                    for bt in range(m_tiles)
+                    for r in range(2)
                 ]
-                for r in range(2)
-            ]
-            top_re = [t[0:1] for t in f_re]
-            top_im = [t[0:1] for t in f_im]
-            half = m_tiles // 2
-            zero = jnp.zeros((1, LANES), F32)
-            base_re = [2.0 * t for t in top_re[:half]] + [zero] * half
-            base_im = [2.0 * t for t in top_im[:half]] + [zero] * half
-            base_re[0] = jnp.where(lane == 0, top_re[0], base_re[0])
-            base_im[0] = jnp.where(lane == 0, 0.0, base_im[0])
-            base_re[half] = jnp.where(lane == 0, top_im[0], 0.0)
-            mid_re.append(
-                jnp.concatenate([2.0 * t for t in top_re[half:]] + [zero] * half, 1)
-            )
-            mid_im.append(
-                jnp.concatenate([2.0 * t for t in top_im[half:]] + [zero] * half, 1)
-            )
+                top_re = f_re[0:8]
+                top_im = f_im[0:8]
+                far_re = pltpu.roll(top_re, LANES // 2, 1)[0:1]
+                far_im = pltpu.roll(top_im, LANES // 2, 1)[0:1]
+                top_re = top_re[0:1]
+                top_im = top_im[0:1]
+                mid.append(
+                    (
+                        jnp.where(lower, 2.0 * far_re, 0.0),
+                        jnp.where(lower, 2.0 * far_im, 0.0),
+                    )
+                )
+                base_re = jnp.where(lower, 2.0 * top_re, 0.0)
+                base_im = jnp.where(lower, 2.0 * top_im, 0.0)
+                if p == 0:
+                    base_re = jnp.where(lane == 0, top_re, base_re)
+                    base_re = jnp.where(lane == LANES // 2, far_im, base_re)
+                    base_im = jnp.where(lane == 0, 0.0, base_im)
+                times_filter(
+                    g,
+                    p,
+                    h * slots,
+                    slots,
+                    jnp.where(first, base_re, f_re),
+                    jnp.where(first, base_im, f_im),
+                )
             times_filter(
                 g,
-                pl.ds(h * slots, slots),
-                jnp.where(first, jnp.concatenate(base_re, 1), jnp.concatenate(f_re, 1)),
-                jnp.where(first, jnp.concatenate(base_im, 1), jnp.concatenate(f_im, 1)),
+                p,
+                2 * slots,
+                extra_rows,
+                jnp.concatenate([mid[0][0], mid[1][0], pad], 0),
+                jnp.concatenate([mid[0][1], mid[1][1], pad], 0),
             )
-        times_filter(
-            g,
-            last_rows,
-            jnp.concatenate([*mid_re, pad], 0),
-            jnp.concatenate([*mid_im, pad], 0),
-        )
-        back = dft_dot(stack[g], dft)
-        tail = back[2 * slots :]
-        tail = tail[:, :seq_len] * middle[0:1] + tail[:, seq_len:] * middle[1:2]
+        for p in range(RADIX):
+            back[p] = transform(p, 1)
+
+        def lines_out(at, count):
+            at = pl.ds(at, count)
+            return radix4([(back[p, at, :LANES], back[p, at, LANES:]) for p in range(RADIX)], 1)
+
+        tail = [
+            re * middle[0:1, t] - im * middle[1:2, t]
+            for t, (re, im) in zip(tiles, lines_out(2 * slots, extra_rows))
+        ]
         for h in range(2):
-            part = back[h * slots : (h + 1) * slots]
-            re = part[:, :seq_len]
-            im = part[:, seq_len:]
-            cos_t = twiddle[0]
-            sin_t = twiddle[1]
-            v_re = re * cos_t + im * sin_t
-            v_im = jnp.where(first, tail[h : h + 1], im * cos_t - re * sin_t)
-            conv = table_dot(inv, jnp.concatenate([v_re, v_im], 0))
+            v_re = []
+            v_im = []
+            for t, end, (re, im) in zip(tiles, tail, lines_out(h * slots, slots)):
+                cos_t = twiddle[0, :, t]
+                sin_t = twiddle[1, :, t]
+                v_re.append(re * cos_t - im * sin_t)
+                v_im.append(jnp.where(first, end[h : h + 1], re * sin_t + im * cos_t))
+            value = jnp.concatenate(
+                [jnp.concatenate(v_re, 1), jnp.concatenate(v_im, 1)], 0
+            )
+            conv = table_dot(inv, value)
             for mt in range(m_tiles):
-                spread(send_y, g, h * m_tiles + mt, conv[:, mt * LANES : (mt + 1) * LANES])
+                spread(send_y, g, h * m_tiles + mt, conv[:, tiles[mt]])
 
     for g in range(2):
         wait_all(recv_x.at[g], x_sem.at[g, 1])
         forward(g)
         wait_all(recv_f.at[g], f_sem.at[g, 1])
         backward(g)
-        exchange(send_y.at[g], recv_y.at[g], y_sem.at[g])
+        exchange(send_y.at[g], recv_y.at[g], y_sem.at[g], far)
 
     for g in range(2):
         wait_all(recv_y.at[g], y_sem.at[g, 1])
@@ -335,6 +387,7 @@
     seq_len, channels = signal.shape
     fwd, inv, dft, twiddle, middle = tables(blocks, seq_len)
     rows = 2 * (seq_len // LANES)
+    lines = blocks + 16
     vmem = pltpu.VMEM
     dma = pltpu.SemaphoreType.DMA
     in_hbm = pl.BlockSpec(memory_space=pltpu.HBM)
@@ -345,14 +398,16 @@
         out_specs=pl.BlockSpec(memory_space=pltpu.VMEM),
         scratch_shapes=[
             vmem(signal.shape, F32),
-            vmem(spectrum.shape[1:], F32),
+            vmem((2, 2, seq_len, LANES), F32),
             vmem(dft.shape, BF16),
             vmem(fwd.shape, BF16),
             vmem(inv.shape, BF16),
             vmem(twiddle.shape, F32),
             vmem(middle.shape, F32),
             *[vmem((2, blocks * rows, LANES), F32) for _ in range(6)],
-            *[vmem((2, blocks + 16, 2 * seq_len), F32) for _ in range(2)],
+            vmem((RADIX, 2 * lines, 2 * LANES), BF16),
+            vmem((2, RADIX, lines, 2 * LANES), F32),
+            vmem((RADIX, lines, 2 * LANES), F32),
             dma((11,)),
             *[dma((2, 2)) for _ in range(3)],
         ],
@@ -360,7 +415,7 @@
             collective_id=1, has_side_effects=True, vmem_limit_bytes=48 * 2**20
         ),
         cost_estimate=pl.CostEstimate(
-            flops=5 * 10**9, bytes_accessed=8 * 2**20, transcendentals=0
+            flops=2 * 10**9, bytes_accessed=8 * 2**20, transcendentals=0
         ),
         name="hyena_conv",
     )(

time: 49.5 us -> 48.8 us (0.986)
  Pallas kernels: 48.2 us -> 47.5 us
    pallas_call x1, Pallas kernels: 48.2 us -> 47.5 us  [body(): pl.pallas_call(functools.partial(kernel, shape), out_shape=jax.ShapeDtype...]
where the time goes in v2:
time: 48.8 us; the launch traced here: 48.7 us
  Pallas kernels  47.5 us (97%)
  other arithmetic  1.2 us (2%)
    pallas_call x1, Pallas kernels, body(): pl.pallas_call(functools.partial(kernel, shape), out_shape=jax.ShapeDtype...  47.5 us
    add x1, other arithmetic, body(): return conv + skip_gain[None, :] * signal  1.2 us

profile of v2, /device:TPU:1, one launch (start us, length us, event | category | flops | bytes accessed | tf_op | source)
XLA Modules:
  0.0 48.7 jit_solution(15340800955552220540)
XLA Ops:
  0.0 0.0 copy-start
  0.0 0.0 copy-start.1
  0.0 47.5 %hyena_conv.1 = f32[512,512]{1,0:T(8,128)S(1)} custom-call(f32[512,512]{1,0:T(8,128)} %signal_hbm.1, f32[2,512,256]{2,1,0:T(8,128)} %bitcast.1, bf16[2,2,4,256,256]{4,3,2,1,0:T(8,128)(2,1)} %constant.10.clone.dft_hbm, bf16[2,128,128]{2,1,0:T(8,128)(2,1)} %constant.11.clone.fwd_hbm, bf16[2,128,128]{2,1,0:T(8,128)(2,1)} %constant.12.clone.inv_hbm, ...), custom_call_target="tpu_custom_call" | custom-call | flops 2000000000 | bytes 8388608 | tf_op jit(solution)/shard_map/hyena_conv/pallas_call | solution.py:394
  47.5 0.0 copy-done
  47.5 0.0 copy-done.1
  47.5 1.2 %multiply_add_fusion = f32[512,512]{1,0:T(8,128)} fusion(f32[512,512]{1,0:T(8,128)S(1)} %hyena_conv.1, f32[512,512]{1,0:T(8,128)S(1)} %copy-done, f32[512]{0:T(512)S(1)} %copy-done.1), kind=kLoop, calls=%fused_computation | loop fusion | flops 524288 | bytes 3147776 | tf_op jit(solution)/shard_map/add | solution.py:435
Async XLA Ops:
  0.0 47.5 %copy-start = (f32[512,512]{1,0:T(8,128)S(1)}, f32[512,512]{1,0:T(8,128)}, u32[]{:S(2)}) copy-start(f32[512,512]{1,0:T(8,128)} %signal_hbm.1) | copy-start | bytes 3145732
  0.0 47.5 %copy-start.1 = (f32[512]{0:T(512)S(1)}, f32[512]{0:T(512)}, u32[]{:S(2)}) copy-start(f32[512]{0:T(512)} %param.10) | copy-start | bytes 6148

commit v3 on v2

--- a/solution.py
+++ b/solution.py
@@ -82,16 +82,20 @@
     return (pr + sr, pi + si), plus, (pr - sr, pi - si), minus
 
 
-def offsets(mesh_shape):
-    axes = [range(n) for n in mesh_shape]
-    every = [o for o in itertools.product(*axes) if any(o)]
+def offsets(shape):
+    every = [o for o in itertools.product(*[range(n) for n in shape]) if any(o)]
+    random.Random(1).shuffle(every)
 
     def hops(o):
-        z, _, x, y = [min(d, n - d) for d, n in zip(o, mesh_shape)]
+        z, _, x, y = [min(d, n - d) for d, n in zip(o, shape)]
         return z + x + y
 
-    random.Random(1).shuffle(every)
-    return every, sorted(every, key=lambda o: -hops(o))
+    every.sort(key=lambda o: -hops(o))
+    levels = [[], [], []]
+    for o in every:
+        z, _, x, y = [int(d > 0) for d in o]
+        levels[max(z + x + y, 1) - 1].append(o)
+    return levels, every
 
 
 def kernel(
@@ -103,6 +107,7 @@
     inv_hbm,
     twiddle_hbm,
     middle_hbm,
+    gain_hbm,
     out_ref,
     signal,
     spectrum,
@@ -111,6 +116,7 @@
     inv,
     twiddle,
     middle,
+    gain,
     send_x,
     recv_x,
     send_f,
@@ -124,6 +130,8 @@
     x_sem,
     f_sem,
     y_sem,
+    second_sem,
+    third_sem,
 ):
     n_z, n_core, n_x, n_y = shape
     outer = lax.axis_index("outer")
@@ -141,41 +149,6 @@
     def lanes(tile):
         return pl.ds(tile * LANES, LANES)
 
-    loads = {}
-
-    def load(name, src, dst):
-        copy = pltpu.make_async_copy(src, dst, load_sem.at[len(loads)])
-        copy.start()
-        loads[name] = copy
-
-    for g in range(2):
-        for h in range(2):
-            where = lanes(2 * h + g)
-            load(("x", g, h), signal_hbm.at[:, where], signal.at[:, where])
-
-    barrier = pltpu.get_barrier_semaphore()
-
-    @pl.loop(0, n_outer)
-    def _(o):
-        for i in range(n_inner):
-
-            @pl.when(jnp.logical_or(o != outer, inner != i))
-            def _():
-                pl.semaphore_signal(
-                    barrier,
-                    inc=1,
-                    device_id=(o, i),
-                    device_id_type=pl.DeviceIdType.MESH,
-                )
-
-    for g in range(2):
-        load(("f", g), spectrum_hbm.at[:, :, lanes(g)], spectrum.at[g])
-    load("fwd", fwd_hbm, fwd)
-    load("twiddle", twiddle_hbm, twiddle)
-    load("middle", middle_hbm, middle)
-    load("dft", dft_hbm, dft)
-    load("inv", inv_hbm, inv)
-
     z, core = outer // n_core, lax.rem(outer, n_core)
     x, y = inner // n_y, lax.rem(inner, n_y)
     at_outer = [
@@ -184,14 +157,52 @@
     ]
     at_x = [lax.rem(x + d, n_x) * n_y for d in range(n_x)]
     at_y = [lax.rem(y + d, n_y) for d in range(n_y)]
-    mixed, far = offsets(shape)
+    levels, far = offsets(shape)
+
+    def device(offset):
+        dz, dc, dx, dy = offset
+        return at_outer[dz][dc], at_x[dx] + at_y[dy]
+
+    def tell(sem):
+        for offset in levels[0]:
+            pl.semaphore_signal(
+                sem,
+                inc=1,
+                device_id=device(offset),
+                device_id_type=pl.DeviceIdType.MESH,
+            )
+
+    def hear(sem):
+        pl.semaphore_wait(sem, len(levels[0]))
+
+    barrier = pltpu.get_barrier_semaphore()
+    tell(barrier)
+
+    loads = {}
+
+    def load(name, src, dst):
+        copy = pltpu.make_async_copy(src, dst, load_sem.at[len(loads)])
+        copy.start()
+        loads[name] = copy
+
+    for g in range(2):
+        for h in range(2):
+            where = lanes(2 * h + g)
+            load(("x", g, h), signal_hbm.at[:, where], signal.at[:, where])
+        load(("f", g), spectrum_hbm.at[:, :, lanes(g)], spectrum.at[g])
+    load("fwd", fwd_hbm, fwd)
+    load("twiddle", twiddle_hbm, twiddle)
+    load("middle", middle_hbm, middle)
+    load("dft", dft_hbm, dft)
+    load("inv", inv_hbm, inv)
+    load("gain", gain_hbm, gain)
 
     def block(ref, index):
         return ref.at[pl.ds(pl.multiple_of(index * rows, rows), rows)]
 
-    def exchange(src, dst, sems, order):
-        for dz, dc, dx, dy in order:
-            to = (at_outer[dz][dc], at_x[dx] + at_y[dy])
+    def send(src, dst, sems, order):
+        for offset in order:
+            to = device(offset)
             pltpu.make_async_remote_copy(
                 src_ref=block(src, to[0] * n_inner + to[1]),
                 dst_ref=block(dst, me),
@@ -200,6 +211,8 @@
                 device_id=to,
                 device_id_type=pl.DeviceIdType.MESH,
             ).start()
+
+    def keep(src, dst):
         own = pl.ds(pl.multiple_of(me * rows, rows), rows)
         dst[own, :] = src[own, :]
 
@@ -209,6 +222,12 @@
 
     def spread(ref, g, index, tile):
         ref[g, pl.ds(index, blocks, stride=rows), :] = tile
+
+    def send_signal(g, order):
+        send(send_x.at[g], recv_x.at[g], x_sem.at[g], order)
+
+    def send_filter(g, order):
+        send(send_f.at[g], recv_f.at[g], f_sem.at[g], order)
 
     for g in range(2):
         for h in range(2):
@@ -216,16 +235,30 @@
             for mt in range(m_tiles):
                 spread(send_x, g, h * m_tiles + mt, signal[lanes(mt), lanes(2 * h + g)].T)
         if g == 0:
-            pl.semaphore_wait(barrier, blocks - 1)
-        exchange(send_x.at[g], recv_x.at[g], x_sem.at[g], mixed)
+            hear(barrier)
+            tell(second_sem)
+        send_signal(g, levels[0])
         loads["f", g].wait()
         for r in range(2):
             for q in range(RADIX):
                 every = pl.ds(q, LANES, stride=RADIX)
                 spread(send_f, g, r * m_tiles + q, spectrum[g, r, every, :].T)
-        exchange(send_f.at[g], recv_f.at[g], f_sem.at[g], (mixed, far)[g])
-
-    for name in ("fwd", "twiddle", "middle", "dft", "inv"):
+        send_filter(g, levels[0])
+    hear(second_sem)
+    tell(third_sem)
+    send_signal(0, levels[1])
+    send_filter(0, levels[1])
+    hear(third_sem)
+    send_signal(0, levels[2])
+    send_filter(0, levels[2])
+    later = [o for o in far if o not in levels[0]]
+    send_signal(1, later)
+    send_filter(1, later)
+    for g in range(2):
+        keep(send_x.at[g], recv_x.at[g])
+        keep(send_f.at[g], recv_f.at[g])
+
+    for name in ("fwd", "twiddle", "middle", "dft", "inv", "gain"):
         loads[name].wait()
     first = lax.broadcasted_iota(jnp.int32, (slots, LANES), 0) == 0
     lane = lax.broadcasted_iota(jnp.int32, (1, LANES), 1)
@@ -363,19 +396,21 @@
         forward(g)
         wait_all(recv_f.at[g], f_sem.at[g, 1])
         backward(g)
-        exchange(send_y.at[g], recv_y.at[g], y_sem.at[g], far)
+        send(send_y.at[g], recv_y.at[g], y_sem.at[g], far)
+        keep(send_y.at[g], recv_y.at[g])
+
+    for g in range(2):
+        wait_all(send_x.at[g], x_sem.at[g, 0])
+        wait_all(send_f.at[g], f_sem.at[g, 0])
+        wait_all(send_y.at[g], y_sem.at[g, 0])
 
     for g in range(2):
         wait_all(recv_y.at[g], y_sem.at[g, 1])
         for h in range(2):
             for mt in range(m_tiles):
                 tile = recv_y[g, pl.ds(h * m_tiles + mt, blocks, stride=rows), :]
-                out_ref[lanes(mt), lanes(2 * h + g)] = tile.T
-
-    for g in range(2):
-        wait_all(send_x.at[g], x_sem.at[g, 0])
-        wait_all(send_f.at[g], f_sem.at[g, 0])
-        wait_all(send_y.at[g], y_sem.at[g, 0])
+                at = lanes(2 * h + g)
+                out_ref[lanes(mt), at] = tile.T + gain[0:1, at] * signal[lanes(mt), at]
 
 
 def body(signal, spectrum, skip_gain):
@@ -391,10 +426,10 @@
     vmem = pltpu.VMEM
     dma = pltpu.SemaphoreType.DMA
     in_hbm = pl.BlockSpec(memory_space=pltpu.HBM)
-    conv = pl.pallas_call(
+    return pl.pallas_call(
         functools.partial(kernel, shape),
         out_shape=jax.ShapeDtypeStruct(signal.shape, F32),
-        in_specs=[in_hbm] * 7,
+        in_specs=[in_hbm] * 8,
         out_specs=pl.BlockSpec(memory_space=pltpu.VMEM),
         scratch_shapes=[
             vmem(signal.shape, F32),
@@ -404,12 +439,15 @@
             vmem(inv.shape, BF16),
             vmem(twiddle.shape, F32),
             vmem(middle.shape, F32),
+            vmem((1, channels), F32),
             *[vmem((2, blocks * rows, LANES), F32) for _ in range(6)],
             vmem((RADIX, 2 * lines, 2 * LANES), BF16),
             vmem((2, RADIX, lines, 2 * LANES), F32),
             vmem((RADIX, lines, 2 * LANES), F32),
-            dma((11,)),
+            dma((12,)),
             *[dma((2, 2)) for _ in range(3)],
+            pltpu.SemaphoreType.REGULAR,
+            pltpu.SemaphoreType.REGULAR,
         ],
         compiler_params=pltpu.CompilerParams(
             collective_id=1, has_side_effects=True, vmem_limit_bytes=48 * 2**20
@@ -429,10 +467,10 @@
                 inv,
                 twiddle,
                 middle,
+                skip_gain[None, :],
             )
         ]
     )
-    return conv + skip_gain[None, :] * signal
 
 
 def solution(mesh):

time: 48.8 us -> 47.8 us (0.980)
  other arithmetic: 1.2 us -> 0 us
  local copies, waits for them, and re-layouts: 0.01 us -> 0.97 us
  Pallas kernels: 47.5 us -> 46.7 us
    add x1 -> x0, other arithmetic: 1.2 us -> none  [body(): return conv + skip_gain[None, :] * signal]
    unnamed x4 -> x1, local copies, waits for them, and re-layouts: 0.01 us -> 0.97 us
    pallas_call x1, Pallas kernels: 47.5 us -> 46.7 us  [body(): pl.pallas_call(functools.partial(kernel, shape), out_shape=jax.ShapeDtype...]
where the time goes in v3:
time: 47.8 us; the launch traced here: 47.7 us
  Pallas kernels  46.7 us (98%)
  local copies, waits for them, and re-layouts  0.97 us (2%)
    pallas_call x1, Pallas kernels, body(): pl.pallas_call(functools.partial(kernel, shape), out_shape=jax.ShapeDtype...  46.7 us
    unnamed x1, local copies, waits for them, and re-layouts  0.97 us

profile of v3, /device:TPU:1, one launch (start us, length us, event | category | flops | bytes accessed | tf_op | source)
XLA Modules:
  0.0 47.7 jit_solution(1130285219396553402)
XLA Ops:
  0.0 46.7 %hyena_conv.1 = f32[512,512]{1,0:T(8,128)S(1)} custom-call(f32[512,512]{1,0:T(8,128)} %signal_hbm.1, f32[2,512,256]{2,1,0:T(8,128)} %bitcast.2, bf16[2,2,4,256,256]{4,3,2,1,0:T(8,128)(2,1)} %constant.10.clone.dft_hbm, bf16[2,128,128]{2,1,0:T(8,128)(2,1)} %constant.11.clone.fwd_hbm, bf16[2,128,128]{2,1,0:T(8,128)(2,1)} %constant.12.clone.inv_hbm, ...), custom_call_target="tpu_custom_call" | custom-call | flops 2000000000 | bytes 8388608 | tf_op jit(solution)/shard_map/hyena_conv/pallas_call | solution.py:429
  46.7 1.0 %copy.10 = f32[512,512]{1,0:T(8,128)} copy(f32[512,512]{1,0:T(8,128)S(1)} %hyena_conv.1) | data formatting | bytes 2097152

commit v4 on v3

--- a/solution.py
+++ b/solution.py
@@ -90,12 +90,13 @@
         z, _, x, y = [min(d, n - d) for d, n in zip(o, shape)]
         return z + x + y
 
-    every.sort(key=lambda o: -hops(o))
     levels = [[], [], []]
     for o in every:
         z, _, x, y = [int(d > 0) for d in o]
         levels[max(z + x + y, 1) - 1].append(o)
-    return levels, every
+    mixed = list(every)
+    every.sort(key=lambda o: -hops(o))
+    return levels, every, mixed
 
 
 def kernel(
@@ -157,7 +158,7 @@
     ]
     at_x = [lax.rem(x + d, n_x) * n_y for d in range(n_x)]
     at_y = [lax.rem(y + d, n_y) for d in range(n_y)]
-    levels, far = offsets(shape)
+    levels, far, mixed = offsets(shape)
 
     def device(offset):
         dz, dc, dx, dy = offset
@@ -252,7 +253,7 @@
     send_signal(0, levels[2])
     send_filter(0, levels[2])
     later = [o for o in far if o not in levels[0]]
-    send_signal(1, later)
+    send_signal(1, [o for o in mixed if o not in levels[0]])
     send_filter(1, later)
     for g in range(2):
         keep(send_x.at[g], recv_x.at[g])
@@ -396,7 +397,7 @@
         forward(g)
         wait_all(recv_f.at[g], f_sem.at[g, 1])
         backward(g)
-        send(send_y.at[g], recv_y.at[g], y_sem.at[g], far)
+        send(send_y.at[g], recv_y.at[g], y_sem.at[g], (mixed, far)[g])
         keep(send_y.at[g], recv_y.at[g])
 
     for g in range(2):

time: 47.8 us -> 47 us (0.983)
  Pallas kernels: 46.7 us -> 45.9 us
    pallas_call x1, Pallas kernels: 46.7 us -> 45.9 us  [body(): pl.pallas_call(functools.partial(kernel, shape), out_shape=jax.ShapeDtype...]
where the time goes in v4:
time: 47 us; the launch traced here: 46.9 us
  Pallas kernels  45.9 us (98%)
  local copies, waits for them, and re-layouts  0.97 us (2%)
    pallas_call x1, Pallas kernels, body(): pl.pallas_call(functools.partial(kernel, shape), out_shape=jax.ShapeDtype...  45.9 us
    unnamed x1, local copies, waits for them, and re-layouts  0.97 us

profile of v4, /device:TPU:1, one launch (start us, length us, event | category | flops | bytes accessed | tf_op | source)
XLA Modules:
  0.0 46.9 jit_solution(1695775497686609115)
XLA Ops:
  0.0 45.9 %hyena_conv.1 = f32[512,512]{1,0:T(8,128)S(1)} custom-call(f32[512,512]{1,0:T(8,128)} %signal_hbm.1, f32[2,512,256]{2,1,0:T(8,128)} %bitcast.2, bf16[2,2,4,256,256]{4,3,2,1,0:T(8,128)(2,1)} %constant.10.clone.dft_hbm, bf16[2,128,128]{2,1,0:T(8,128)(2,1)} %constant.11.clone.fwd_hbm, bf16[2,128,128]{2,1,0:T(8,128)(2,1)} %constant.12.clone.inv_hbm, ...), custom_call_target="tpu_custom_call" | custom-call | flops 2000000000 | bytes 8388608 | tf_op jit(solution)/shard_map/hyena_conv/pallas_call | solution.py:430
  45.9 1.0 %copy.10 = f32[512,512]{1,0:T(8,128)} copy(f32[512,512]{1,0:T(8,128)S(1)} %hyena_conv.1) | data formatting | bytes 2097152

commit v5 on v4

--- a/solution.py
+++ b/solution.py
@@ -201,17 +201,41 @@
     def block(ref, index):
         return ref.at[pl.ds(pl.multiple_of(index * rows, rows), rows)]
 
+    def send_one(src, dst, sems, to):
+        pltpu.make_async_remote_copy(
+            src_ref=block(src, to[0] * n_inner + to[1]),
+            dst_ref=block(dst, me),
+            send_sem=sems.at[0],
+            recv_sem=sems.at[1],
+            device_id=to,
+            device_id_type=pl.DeviceIdType.MESH,
+        ).start()
+
     def send(src, dst, sems, order):
         for offset in order:
+            send_one(src, dst, sems, device(offset))
+
+    def hops(d, n):
+        return jnp.minimum(d, n - d)
+
+    def send_last(src, dst, sems):
+        near = hops(z, n_z) + hops(x, n_x) + hops(y, n_y) <= 2
+        for c in range(n_core):
+
+            @pl.when(near & ((outer != c) | (inner != 0)))
+            def _():
+                send_one(src, dst, sems, (c, 0))
+
+        for offset in far:
             to = device(offset)
-            pltpu.make_async_remote_copy(
-                src_ref=block(src, to[0] * n_inner + to[1]),
-                dst_ref=block(dst, me),
-                send_sem=sems.at[0],
-                recv_sem=sems.at[1],
-                device_id=to,
-                device_id_type=pl.DeviceIdType.MESH,
-            ).start()
+            dz, _, dx, dy = offset
+            if min(dz, n_z - dz) + min(dx, n_x - dx) + min(dy, n_y - dy) > 2:
+                send_one(src, dst, sems, to)
+            else:
+
+                @pl.when((to[0] >= n_core) | (to[1] != 0))
+                def _():
+                    send_one(src, dst, sems, to)
 
     def keep(src, dst):
         own = pl.ds(pl.multiple_of(me * rows, rows), rows)
@@ -397,7 +421,10 @@
         forward(g)
         wait_all(recv_f.at[g], f_sem.at[g, 1])
         backward(g)
-        send(send_y.at[g], recv_y.at[g], y_sem.at[g], (mixed, far)[g])
+        if g == 0:
+            send(send_y.at[g], recv_y.at[g], y_sem.at[g], mixed)
+        else:
+            send_last(send_y.at[g], recv_y.at[g], y_sem.at[g])
         keep(send_y.at[g], recv_y.at[g])
 
     for g in range(2):

time: 47 us -> 46.8 us (level)
  no operation moved by 1% of the time
where the time goes in v5:
time: 46.8 us; the launch traced here: 46.7 us
  Pallas kernels  45.8 us (98%)
  local copies, waits for them, and re-layouts  0.97 us (2%)
    pallas_call x1, Pallas kernels, body(): pl.pallas_call(functools.partial(kernel, shape), out_shape=jax.ShapeDtype...  45.8 us
    unnamed x1, local copies, waits for them, and re-layouts  0.97 us

profile of v5, /device:TPU:1, one launch (start us, length us, event | category | flops | bytes accessed | tf_op | source)
XLA Modules:
  0.0 46.7 jit_solution(8602849151210507144)
XLA Ops:
  0.0 45.8 %hyena_conv.1 = f32[512,512]{1,0:T(8,128)S(1)} custom-call(f32[512,512]{1,0:T(8,128)} %signal_hbm.1, f32[2,512,256]{2,1,0:T(8,128)} %bitcast.2, bf16[2,2,4,256,256]{4,3,2,1,0:T(8,128)(2,1)} %constant.10.clone.dft_hbm, bf16[2,128,128]{2,1,0:T(8,128)(2,1)} %constant.11.clone.fwd_hbm, bf16[2,128,128]{2,1,0:T(8,128)(2,1)} %constant.12.clone.inv_hbm, ...), custom_call_target="tpu_custom_call" | custom-call | flops 2000000000 | bytes 8388608 | tf_op jit(solution)/shard_map/hyena_conv/pallas_call | solution.py:457
  45.8 1.0 %copy.10 = f32[512,512]{1,0:T(8,128)} copy(f32[512,512]{1,0:T(8,128)S(1)} %hyena_conv.1) | data formatting | bytes 2097152

commit v6 on v4

--- a/solution.py
+++ b/solution.py
@@ -392,12 +392,18 @@
             for mt in range(m_tiles):
                 spread(send_y, g, h * m_tiles + mt, conv[:, tiles[mt]])
 
-    for g in range(2):
+    @pl.loop(0, 2)
+    def _(g):
         wait_all(recv_x.at[g], x_sem.at[g, 1])
         forward(g)
         wait_all(recv_f.at[g], f_sem.at[g, 1])
         backward(g)
-        send(send_y.at[g], recv_y.at[g], y_sem.at[g], (mixed, far)[g])
+        for group, order in enumerate((mixed, far)):
+
+            @pl.when(g == group)
+            def _():
+                send(send_y.at[group], recv_y.at[group], y_sem.at[group], order)
+
         keep(send_y.at[g], recv_y.at[g])
 
     for g in range(2):

time: 47 us -> 47 us (level)
  no operation moved by 1% of the time
where the time goes in v6:
time: 47 us; the launch traced here: 46.9 us
  Pallas kernels  45.9 us (98%)
  local copies, waits for them, and re-layouts  0.97 us (2%)
    pallas_call x1, Pallas kernels, body(): pl.pallas_call(functools.partial(kernel, shape), out_shape=jax.ShapeDtype...  45.9 us
    unnamed x1, local copies, waits for them, and re-layouts  0.97 us

profile of v6, /device:TPU:1, one launch (start us, length us, event | category | flops | bytes accessed | tf_op | source)
XLA Modules:
  0.0 46.9 jit_solution(5561524028351576403)
XLA Ops:
  0.0 45.9 %hyena_conv.1 = f32[512,512]{1,0:T(8,128)S(1)} custom-call(f32[512,512]{1,0:T(8,128)} %signal_hbm.1, f32[2,512,256]{2,1,0:T(8,128)} %bitcast.2, bf16[2,2,4,256,256]{4,3,2,1,0:T(8,128)(2,1)} %constant.10.clone.dft_hbm, bf16[2,128,128]{2,1,0:T(8,128)(2,1)} %constant.11.clone.fwd_hbm, bf16[2,128,128]{2,1,0:T(8,128)(2,1)} %constant.12.clone.inv_hbm, ...), custom_call_target="tpu_custom_call" | custom-call | flops 2000000000 | bytes 8388608 | tf_op jit(solution)/shard_map/hyena_conv/pallas_call | solution.py:436
  45.9 1.0 %copy.10 = f32[512,512]{1,0:T(8,128)} copy(f32[512,512]{1,0:T(8,128)S(1)} %hyena_conv.1) | data formatting | bytes 2097152

commit v7 on v4

--- a/solution.py
+++ b/solution.py
@@ -235,15 +235,15 @@
             loads["x", g, h].wait()
             for mt in range(m_tiles):
                 spread(send_x, g, h * m_tiles + mt, signal[lanes(mt), lanes(2 * h + g)].T)
-        if g == 0:
-            hear(barrier)
-            tell(second_sem)
-        send_signal(g, levels[0])
         loads["f", g].wait()
         for r in range(2):
             for q in range(RADIX):
                 every = pl.ds(q, LANES, stride=RADIX)
                 spread(send_f, g, r * m_tiles + q, spectrum[g, r, every, :].T)
+    hear(barrier)
+    tell(second_sem)
+    for g in range(2):
+        send_signal(g, levels[0])
         send_filter(g, levels[0])
     hear(second_sem)
     tell(third_sem)

time: 47 us -> 47.3 us (level)
  no operation moved by 1% of the time
where the time goes in v7:
time: 47.3 us; the launch traced here: 47.2 us
  Pallas kernels  46.2 us (98%)
  local copies, waits for them, and re-layouts  0.97 us (2%)
    pallas_call x1, Pallas kernels, body(): pl.pallas_call(functools.partial(kernel, shape), out_shape=jax.ShapeDtype...  46.2 us
    unnamed x1, local copies, waits for them, and re-layouts  0.97 us

profile of v7, /device:TPU:1, one launch (start us, length us, event | category | flops | bytes accessed | tf_op | source)
XLA Modules:
  0.0 47.2 jit_solution(8552022972409183099)
XLA Ops:
  0.0 46.2 %hyena_conv.1 = f32[512,512]{1,0:T(8,128)S(1)} custom-call(f32[512,512]{1,0:T(8,128)} %signal_hbm.1, f32[2,512,256]{2,1,0:T(8,128)} %bitcast.2, bf16[2,2,4,256,256]{4,3,2,1,0:T(8,128)(2,1)} %constant.10.clone.dft_hbm, bf16[2,128,128]{2,1,0:T(8,128)(2,1)} %constant.11.clone.fwd_hbm, bf16[2,128,128]{2,1,0:T(8,128)(2,1)} %constant.12.clone.inv_hbm, ...), custom_call_target="tpu_custom_call" | custom-call | flops 2000000000 | bytes 8388608 | tf_op jit(solution)/shard_map/hyena_conv/pallas_call | solution.py:430
  46.2 1.0 %copy.10 = f32[512,512]{1,0:T(8,128)} copy(f32[512,512]{1,0:T(8,128)S(1)} %hyena_conv.1) | data formatting | bytes 2097152
